TPU v7x, 256 devices: a whole 4x4x8 slice. The times are simulated.
256 devices in a mesh: loop: 32 (over z, x_hi, core), bcast: 8 (over y, x_lo).
Axes of the slice: x: 4 (x_hi: 2, x_lo: 2; x = x_hi * 2 + x_lo), y: 4, z: 8, core: 2. Of those that a mesh axis runs over, the one named last changes fastest.
Arguments:
- s_blocks: float32 [32, 8, 1, 10, 256, 256], P('loop', 'bcast'), may hold values from -6 to 6
- s_list: int32 [32, 8, 1, 10, 2], P('loop', 'bcast'), may hold values from 0 to 3, as said below
- x_blocks: float32 [32, 8, 12, 256, 256], P('loop', 'bcast'), may hold values from -0.09375 to 0.09375
- x_list: int32 [32, 8, 12, 2], P('loop', 'bcast'), may hold values from 0 to 4, as said below
- c_list: int32 [32, 8, 10, 2], P('loop', 'bcast'), may hold values from 0 to 3, as said below
- owner: int32 [32, 4], P('loop'), may hold values from 0 to 7, as said below
Outputs:
- product: float32 [32, 8, 10, 256, 256], P('loop', 'bcast')
Inputs may be any that keep to these rules, and one draw needn't show every extreme that they name: `s_list`: positions within one list are distinct. `x_list`: positions within one list are distinct; entries with first value 4 are empty and stand after the occupied ones; some device's list has no empty entry. `c_list`: positions within one list are distinct. owner[l, s] = (s + q_l) mod 8 for a whole number q_l of each block-row group.
All inputs are finite; a program needn't handle non-finite values.
Results may differ from a plain program's by a relative error of at most 0.0003.
Values sent between devices are 32-bit elements; how exact they have to be, the bound alone decides.
A program may use at most 192 MiB of HBM per device.

v0:
```python
import jax
import jax.numpy as jnp
from jax import lax
from jax.sharding import PartitionSpec as P

RB = 3
KB = 4
CB = 4
STEPS = 4
HIGHEST = lax.Precision.HIGHEST


def shifted(shard, axis, by):
    length = lax.axis_size(axis)
    return lax.ppermute(shard, axis, [(i, (i + by) % length) for i in range(length)])


def spread(block, axis, owner):
    block = jnp.where(lax.axis_index(axis) == owner, block, jnp.zeros_like(block))
    return lax.psum(block, axis)


def densify(blocks, places, row_count, col_count):
    whole = places.astype(jnp.int32)
    chosen = (whole[:, 0][:, None, None] == jnp.arange(row_count)[None, :, None]) & (
        whole[:, 1][:, None, None] == jnp.arange(col_count)[None, None, :]
    )
    return jnp.einsum("irc,iab->rcab", chosen.astype(jnp.float32), blocks, precision=HIGHEST)


def block_terms(left, right, pairs):
    full_slab = jnp.einsum("rkab,kcbd->rcad", left, right, precision=HIGHEST)
    return full_slab[pairs[:, 0], pairs[:, 1]]


def per_device(s_blocks, s_list, x_blocks, x_list, c_list, owner):
    width = lax.axis_size("bcast")
    pairs = c_list[0, 0]
    resident = (x_blocks[0, 0], x_list[0, 0].astype(jnp.float32))
    current = resident
    total = jnp.zeros((pairs.shape[0], x_blocks.shape[3], x_blocks.shape[4]), jnp.float32)
    for step in range(STEPS):
        if step > 0:
            current = shifted((current[0], current[1]), "loop", -1)
        root = owner[0, step]
        slot = step // width
        left_blocks, left_places = (
            spread(s_blocks[0, 0, slot], "bcast", root),
            spread(s_list[0, 0, slot].astype(jnp.float32), "bcast", root),
        )
        left = densify(left_blocks, left_places, RB, KB)
        right = densify(current[0], current[1], KB, CB)
        total = total + block_terms(left, right, pairs)
    return total[None, None]


def solution(mesh):
    return jax.shard_map(
        per_device,
        mesh=mesh,
        in_specs=(
            P("loop", "bcast", None, None, None, None),
            P("loop", "bcast", None, None, None),
            P("loop", "bcast", None, None, None),
            P("loop", "bcast", None, None),
            P("loop", "bcast", None, None),
            P("loop", None),
        ),
        out_specs=P("loop", "bcast", None, None, None),
        check_vma=False,
    )
```

profile of v0, /device:TPU:1, one launch (start us, length us, event | category | flops | bytes accessed | tf_op | source)
XLA Modules:
  0.0 678.7 jit_solution(14331984064396226932)
XLA Ops:
  6.5 1.5 fusion.79
  10.5 6.0 select_bitcast_fusion.2
  16.5 1.9 copy-done.4
  18.4 3.2 collective-permute-start.1
  21.6 6.0 collective-permute-start
  27.7 42.8 %all-reduce = (f32[10,2]{0,1:T(2,128)S(1)}, f32[10,2]{0,1:T(2,128)S(1)}, f32[10,2]{0,1:T(2,128)S(1)}, f32[10,2]{0,1:T(2,128)S(1)}) all-reduce(f32[10,2]{0,1:T(2,128)S(1)} %get-tuple-element.37, f32[10,2]{0,1:T(2,128)S(1)} %get-tuple-element.36, f32[10,2]{0,1:T(2,128)S(1)} %get-tuple-element.38, ...), channel_id=1, replica_groups=mesh['loop'=32,'bcast'=8] {'bcast'}, use_global_device_ids=true, to_apply=%region_6.7 | all-reduce | flops 80 | bytes 640 | tf_op jit(solution)/shard_map/psum | solution.py:20
  70.5 33.0 %collective-permute-done.1 = f32[12,256,256]{2,1,0:T(8,128)} collective-permute-done((f32[12,256,256]{2,1,0:T(8,128)S(1)}, f32[12,256,256]{2,1,0:T(8,128)}, u32[]{:S(2)}, u32[]{:S(2)}) %collective-permute-start.1) | collective-permute-done | bytes 3145760 | tf_op jit(solution)/shard_map/ppermute | solution.py:15
  103.5 0.1 iota_compare_fusion
  103.6 0.1 iota_compare_fusion.1
  103.6 0.1 iota_compare_fusion.4
  103.7 0.1 iota_compare_fusion.5
  103.8 0.1 iota_compare_fusion.8
  103.9 0.1 iota_compare_fusion.9
  104.2 0.1 and_bitcast_fusion.4
  104.2 0.1 and_bitcast_fusion.5
  104.3 0.1 and_bitcast_fusion.6
  104.4 0.1 and_bitcast_fusion.3
  104.5 118.5 %collective-permute-done.3 = f32[12,256,256]{2,1,0:T(8,128)S(1)} collective-permute-done((f32[12,256,256]{2,1,0:T(8,128)}, f32[12,256,256]{2,1,0:T(8,128)S(1)}, u32[]{:S(2)}, u32[]{:S(2)}) %collective-permute-start.3) | collective-permute-done | bytes 3145760 | tf_op jit(solution)/shard_map/ppermute | solution.py:15
  223.0 0.1 and_bitcast_fusion.7
  223.1 6.2 fusion.32
  229.3 0.1 collective-permute-start.2
  229.4 0.1 iota_compare_fusion.10
  229.5 0.1 and_bitcast_fusion.2
  229.6 93.1 %collective-permute-done.2 = f32[12,2]{0,1:T(2,128)S(1)} collective-permute-done((f32[12,2]{0,1:T(2,128)S(1)}, f32[12,2]{0,1:T(2,128)S(1)}, u32[]{:S(2)}, u32[]{:S(2)}) %collective-permute-start.2) | collective-permute-done | bytes 128 | tf_op jit(solution)/shard_map/ppermute | solution.py:15
  322.7 0.4 collective-permute-start.4
  323.2 0.1 iota_compare_fusion.6
  323.2 0.1 and_bitcast_fusion.1
  323.3 4.3 collective-permute-done.4
  327.6 0.1 iota_compare_fusion.2
  327.7 0.1 and_bitcast_fusion
  327.8 8.3 %fusion.35 = f32[4,4,256,256,1]{3,1,2,0,4:T(4,128)} fusion(f32[12,256,256,1]{2,1,0,3:T(8,128)} %bitcast.23, pred[12,4,4,1]{2,1,0,3:T(4,128)(4,1)S(1)} %and_bitcast_fusion.2), kind=kOutput, calls=%fused_computation.42 | convolution fusion | flops 150994944 | bytes 7340224 | tf_op jit(solution)/shard_map/irc,iab->rcab/dot_general | solution.py:28
  336.1 6.2 fusion.38
  342.3 6.1 fusion.41
  348.5 200.5 %all-reduce.4.cloned.1.call-done = (f32[10,256,256]{2,1,0:T(8,128)}, f32[10,256,256]{2,1,0:T(8,128)}, f32[10,256,256]{2,1,0:T(8,128)}, f32[10,256,256]{2,1,0:T(8,128)}) async-done(((f32[10,256,256]{2,1,0:T(8,128)}, f32[10,256,256]{2,1,0:T(8,128)}, f32[10,256,256]{2,1,0:T(8,128)}, f32[10,256,256]{2,1,0:T(8,128)}), (f32[10,256,256]{2,1,0:T(8,128)}, f32[10,256,256]{2,1,0:T(8,128)}, f32[10,256,256]{2,1,0:T(8,128)}, ...) | async-done | bytes 10485776 | tf_op jit(solution)/shard_map/psum | solution.py:20
  548.9 6.2 fusion.8
  555.2 20.2 %fusion.59 = f32[3,4,256,256]{2,3,0,1:T(8,128)S(1)} fusion(f32[3,4,256,256]{3,1,2,0:T(4,128)S(1)} %fusion.8, f32[4,4,256,256,1]{3,1,2,0,4:T(4,128)S(1)} %copy-done.3), kind=kOutput, calls=%fused_computation.48 | convolution fusion | flops 9663676416 | bytes 10485760 | tf_op jit(solution)/shard_map/rkab,kcbd->rcad/dot_general | solution.py:32
  575.4 2.3 gather_fusion.3
  577.7 6.5 fusion.12
  584.2 20.2 %fusion.54 = f32[3,4,256,256]{2,3,0,1:T(8,128)S(1)} fusion(f32[3,4,256,256]{3,1,2,0:T(4,128)S(1)} %fusion.12, f32[4,4,256,256,1]{3,1,2,0,4:T(4,128)S(1)} %copy-done.2), kind=kOutput, calls=%fused_computation.47 | convolution fusion | flops 9663676416 | bytes 10485760 | tf_op jit(solution)/shard_map/rkab,kcbd->rcad/dot_general | solution.py:32
  604.4 2.4 gather_fusion.2
  606.8 6.3 fusion.16
  613.1 20.4 %fusion.49 = f32[3,4,256,256]{2,3,0,1:T(8,128)S(1)} fusion(f32[3,4,256,256]{3,1,2,0:T(4,128)S(1)} %fusion.16, f32[4,4,256,256,1]{3,1,2,0,4:T(4,128)S(1)} %copy-done.1), kind=kOutput, calls=%fused_computation.46 | convolution fusion | flops 9663676416 | bytes 10485760 | tf_op jit(solution)/shard_map/rkab,kcbd->rcad/dot_general | solution.py:32
  633.5 2.3 gather_fusion.1
  635.9 6.3 fusion.20
  642.1 20.2 %fusion.44 = f32[3,4,256,256]{2,3,0,1:T(8,128)S(1)} fusion(f32[3,4,256,256]{3,1,2,0:T(4,128)S(1)} %fusion.20, f32[4,4,256,256,1]{3,1,2,0,4:T(4,128)S(1)} %copy-done), kind=kOutput, calls=%fused_computation.45 | convolution fusion | flops 9663676416 | bytes 10485760 | tf_op jit(solution)/shard_map/rkab,kcbd->rcad/dot_general | solution.py:32
  662.4 2.3 gather_fusion
  664.7 4.9 add_bitcast_fusion
  669.6 2.1 copy.7
  (42 shorter events, 0.4 us)
Async XLA Ops:
  6.5 542.4 %all-reduce.4.cloned.1.call-start = ((), (), s32[]{:S(2)}) async-start(), calls=%async_computation | async-start | bytes 20971520 | tf_op jit(solution)/shard_map/psum | solution.py:20
  16.5 1.9 copy-start.4
  16.5 5.1 copy-start.5
  16.5 11.2 %copy-start.6 = (s32[1,1,1,10,2]{3,4,2,1,0:T(2,128)S(1)}, s32[1,1,1,10,2]{3,4,2,1,0:T(2,128)}, u32[]{:S(2)}) copy-start(s32[1,1,1,10,2]{3,4,2,1,0:T(2,128)} %param.7) | copy-start | bytes 244
  18.4 85.1 %collective-permute-start.1 = (f32[12,256,256]{2,1,0:T(8,128)S(1)}, f32[12,256,256]{2,1,0:T(8,128)}, u32[]{:S(2)}, u32[]{:S(2)}) collective-permute-start(f32[12,256,256]{2,1,0:T(8,128)S(1)} %bitcast.139), channel_id=1, source_target_pairs={{0,248},{8,0},{16,8},{24,16},{32,24},{40,32},{48,40},{56,48},{64,5... | collective-permute-start | bytes 9437192 | tf_op jit(solution)/shard_map/ppermute | solution.py:15
  21.6 207.7 %collective-permute-start = (f32[12,2]{0,1:T(2,128)S(1)}, f32[12,2]{0,1:T(2,128)S(1)}, u32[]{:S(2)}, u32[]{:S(2)}) collective-permute-start(f32[12,2]{0,1:T(2,128)S(1)} %get-tuple-element.24), channel_id=1, source_target_pairs={{0,248},{8,0},{16,8},{24,16},{32,24},{40,32},{48,40},{56,48},{64,5... | collective-permute-start | bytes 296 | tf_op jit(solution)/shard_map/ppermute | solution.py:15
  103.5 119.5 %collective-permute-start.3 = (f32[12,256,256]{2,1,0:T(8,128)}, f32[12,256,256]{2,1,0:T(8,128)S(1)}, u32[]{:S(2)}, u32[]{:S(2)}) collective-permute-start(f32[12,256,256]{2,1,0:T(8,128)} %collective-permute-done.1), channel_id=1, source_target_pairs={{0,248},{8,0},{16,8},{24,16},{32,24},{40,32},{48,40},{56,48},{64,5... | collective-permute-start | bytes 9437192 | tf_op jit(solution)/shard_map/ppermute | solution.py:15
  223.0 119.3 %collective-permute-start.5 = (f32[12,256,256]{2,1,0:T(8,128)S(1)}, f32[12,256,256]{2,1,0:T(8,128)S(1)}, u32[]{:S(2)}, u32[]{:S(2)}) collective-permute-start(f32[12,256,256]{2,1,0:T(8,128)S(1)} %collective-permute-done.3), channel_id=1, source_target_pairs={{0,248},{8,0},{16,8},{24,16},{32,24},{40,32},{48,40},{56,48},{64,5... | collective-permute-start | bytes 9437192 | tf_op jit(solution)/shard_map/ppermute | solution.py:15
  223.1 6.2 copy-start.7
  229.3 93.4 %collective-permute-start.2 = (f32[12,2]{0,1:T(2,128)S(1)}, f32[12,2]{0,1:T(2,128)S(1)}, u32[]{:S(2)}, u32[]{:S(2)}) collective-permute-start(f32[12,2]{0,1:T(2,128)S(1)} %collective-permute-done), channel_id=1, source_target_pairs={{0,248},{8,0},{16,8},{24,16},{32,24},{40,32},{48,40},{56,48},{64,5... | collective-permute-start | bytes 296 | tf_op jit(solution)/shard_map/ppermute | solution.py:15
  322.7 4.9 collective-permute-start.4
  548.9 6.3 copy-start.3
  577.7 6.5 copy-start.2
  606.8 6.3 copy-start.1
  635.9 6.3 copy-start
Sparse Core Ops, SparseCore 0:
  16.6 532.2 all-reduce.3
where the time goes:
time: 685 us; the launch traced here: 679 us
  waiting for transfers between devices  449 us (66%)
  matrix products  133 us (19%)
  blocking collectives  42.8 us (6%)
  between operations  16.4 us (2%)
  local copies, waits for them, and re-layouts  14.9 us (2%)
  other arithmetic  12.4 us (2%)
  starting transfers between devices  9.8 us (1%)
    ppermute x6, waiting for transfers between devices, shifted(): lax.ppermute(shard, axis, [(i, (i + by) % length) for i in range(length)])  249 us
    psum x1, waiting for transfers between devices, spread(): return lax.psum(block, axis)  200 us
    dot_general x4, matrix products, block_terms(): full_slab = jnp.einsum('rkab,kcbd->rcad', left, right, precision=HIGHEST)  81 us
    dot_general x8, matrix products, densify(): jnp.einsum('irc,iab->rcab', chosen.astype(jnp.float32), blocks, precision...  52.1 us
    psum x1, blocking collectives, spread(): return lax.psum(block, axis)  42.8 us
  transfers between devices with their start and end apart: 7, of which 5 were waited for; matrix products, arithmetic and copies ran while one was open for 4% of the time, Pallas kernels for 0%

commit v1 on v0

--- a/solution.py
+++ b/solution.py
@@ -17,7 +17,7 @@
 
 def spread(block, axis, owner):
     block = jnp.where(lax.axis_index(axis) == owner, block, jnp.zeros_like(block))
-    return lax.psum(block, axis)
+    return jnp.sum(lax.all_gather(block, axis), axis=0)
 
 
 def densify(blocks, places, row_count, col_count):

time: 685 us -> 1810 us (2.64)
  waiting for transfers between devices: 449 us -> 1470 us
  blocking collectives: 42.8 us -> 81.5 us
  other arithmetic: 12.4 us -> 45.2 us
  starting transfers between devices: 9.8 us -> 40.6 us
    all_gather x0 -> x4, waiting for transfers between devices: none -> 1240 us  [spread(): return jnp.sum(lax.all_gather(block, axis), axis=0)]
    psum x1 -> x0, waiting for transfers between devices: 200 us -> none  [spread(): return lax.psum(block, axis)]
    all_gather x0 -> x4, blocking collectives: none -> 81.5 us  [spread(): return jnp.sum(lax.all_gather(block, axis), axis=0)]
    psum x1 -> x0, blocking collectives: 42.8 us -> none  [spread(): return lax.psum(block, axis)]
    reduce_sum x0 -> x8, other arithmetic: none -> 32.7 us  [spread(): return jnp.sum(lax.all_gather(block, axis), axis=0)]
    ppermute x6, starting transfers between devices: 9.8 us -> 40.5 us  [shifted(): lax.ppermute(shard, axis, [(i, (i + by) % length) for i in range(length)])]
    ppermute x6, waiting for transfers between devices: 249 us -> 229 us  [shifted(): lax.ppermute(shard, axis, [(i, (i + by) % length) for i in range(length)])]
  transfers between devices with their start and end apart: 7 -> 10, of which waited for: 5 -> 8; matrix products, arithmetic and copies ran while one was open for 4% -> 8% of each run, Pallas kernels for 0% -> 0%
where the time goes in v1:
time: 1810 us; the launch traced here: 1800 us
  waiting for transfers between devices  1470 us (81%)
  matrix products  128 us (7%)
  blocking collectives  81.5 us (5%)
  other arithmetic  45.2 us (2%)
  starting transfers between devices  40.6 us (2%)
    all_gather x4, waiting for transfers between devices, spread(): return jnp.sum(lax.all_gather(block, axis), axis=0)  1240 us
    ppermute x6, waiting for transfers between devices, shifted(): lax.ppermute(shard, axis, [(i, (i + by) % length) for i in range(length)])  229 us
    all_gather x4, blocking collectives, spread(): return jnp.sum(lax.all_gather(block, axis), axis=0)  81.5 us
    dot_general x4, matrix products, block_terms(): full_slab = jnp.einsum('rkab,kcbd->rcad', left, right, precision=HIGHEST)  81 us
    dot_general x8, matrix products, densify(): jnp.einsum('irc,iab->rcab', chosen.astype(jnp.float32), blocks, precision...  46.9 us
    ppermute x6, starting transfers between devices, shifted(): lax.ppermute(shard, axis, [(i, (i + by) % length) for i in range(length)])  40.5 us
  transfers between devices with their start and end apart: 10, of which 8 were waited for; matrix products, arithmetic and copies ran while one was open for 8% of the time, Pallas kernels for 0%

profile of v1, /device:TPU:1, one launch (start us, length us, event | category | flops | bytes accessed | tf_op | source)
XLA Modules:
  0.0 1799.9 jit_solution(9038650741435574685)
XLA Ops:
  6.5 1.5 fusion.79
  10.6 6.0 broadcast_select_fusion.2
  16.7 0.7 all-gather.17.cloned.1.call-update
  17.5 0.7 all-gather.13.cloned.1.call-update
  18.2 0.5 all-gather.15.cloned.1.call-update
  18.7 0.5 copy-done.4
  19.3 3.2 collective-permute-start.1
  22.5 6.0 collective-permute-start
  28.6 41.3 %all-gather.6 = f32[8,1,1,10,2]{3,4,2,1,0:T(2,128)S(1)} all-gather(f32[1,1,1,10,2]{3,4,2,1,0:T(2,128)S(1)} %get-tuple-element.15), channel_id=8, replica_groups=mesh['loop'=32,'bcast'=8] {'bcast'}, dimensions={0}, use_global_device_ids=true | all-gather | bytes 720 | tf_op jit(solution)/shard_map/all_gather | solution.py:20
  69.9 12.9 all-gather.4
  82.8 13.9 all-gather
  96.8 8.4 collective-permute-done.1
  105.2 30.7 %collective-permute-start.3 = (f32[12,256,256]{2,1,0:T(8,128)}, f32[12,256,256]{2,1,0:T(8,128)}, u32[]{:S(2)}, u32[]{:S(2)}) collective-permute-start(f32[12,256,256]{2,1,0:T(8,128)} %collective-permute-done.1), channel_id=1, source_target_pairs={{0,248},{8,0},{16,8},{24,16},{32,24},{40,32},{48,40},{56,48},{64,5... | collective-permute-start | bytes 9437192 | tf_op jit(solution)/shard_map/ppermute | solution.py:15
  135.9 13.4 all-gather.2
  150.0 0.1 and_bitcast_fusion.4
  150.3 0.1 and_bitcast_fusion.3
  150.4 105.9 %collective-permute-done.3 = f32[12,256,256]{2,1,0:T(8,128)} collective-permute-done((f32[12,256,256]{2,1,0:T(8,128)}, f32[12,256,256]{2,1,0:T(8,128)}, u32[]{:S(2)}, u32[]{:S(2)}) %collective-permute-start.3) | collective-permute-done | bytes 3145760 | tf_op jit(solution)/shard_map/ppermute | solution.py:15
  256.4 6.2 fusion.32
  262.5 0.1 collective-permute-start.2
  262.8 110.7 %collective-permute-done.2 = f32[12,2]{0,1:T(2,128)S(1)} collective-permute-done((f32[12,2]{0,1:T(2,128)S(1)}, f32[12,2]{0,1:T(2,128)S(1)}, u32[]{:S(2)}, u32[]{:S(2)}) %collective-permute-start.2) | collective-permute-done | bytes 128 | tf_op jit(solution)/shard_map/ppermute | solution.py:15
  373.5 0.4 collective-permute-start.4
  374.2 4.3 collective-permute-done.4
  378.6 0.1 and_bitcast_fusion
  378.7 8.3 fusion.35
  387.0 8.3 fusion.38
  395.3 6.2 fusion.41
  401.5 119.9 %all-gather.19.cloned.1.call-done = f32[8,1,1,10,256,256]{5,4,3,2,1,0:T(8,128)} async-done(((f32[1,1,1,10,256,256]{5,4,3,2,1,0:T(8,128)}), f32[8,1,1,10,256,256]{5,4,3,2,1,0:T(8,128)}) %all-gather.19.cloned.1.call-update) | async-done | bytes 20971536 | tf_op jit(solution)/shard_map/all_gather | solution.py:20
  521.4 8.2 reduce_sum.79
  529.6 4.4 fusion.8
  534.0 20.2 %fusion.59 = f32[3,4,256,256]{2,3,0,1:T(8,128)S(1)} fusion(f32[3,4,256,256]{3,1,2,0:T(4,128)S(1)} %fusion.8, f32[4,4,256,256,1]{3,1,2,0,4:T(4,128)S(1)} %copy-done.3), kind=kOutput, calls=%fused_computation.44 | convolution fusion | flops 9663676416 | bytes 10485760 | tf_op jit(solution)/shard_map/rkab,kcbd->rcad/dot_general | solution.py:32
  554.2 2.4 gather_fusion.3
  556.6 375.3 %all-gather.17.cloned.1.call-done = f32[8,1,1,10,256,256]{5,4,3,2,1,0:T(8,128)} async-done(((f32[1,1,1,10,256,256]{5,4,3,2,1,0:T(8,128)}), f32[8,1,1,10,256,256]{5,4,3,2,1,0:T(8,128)}) %all-gather.17.cloned.1.call-update) | async-done | bytes 20971536 | tf_op jit(solution)/shard_map/all_gather | solution.py:20
  931.9 8.2 reduce_sum.77
  940.0 4.7 fusion.12
  944.7 20.2 %fusion.54 = f32[3,4,256,256]{2,3,0,1:T(8,128)S(1)} fusion(f32[3,4,256,256]{3,1,2,0:T(4,128)S(1)} %fusion.12, f32[4,4,256,256,1]{3,1,2,0,4:T(4,128)S(1)} %copy-done.2), kind=kOutput, calls=%fused_computation.43 | convolution fusion | flops 9663676416 | bytes 10485760 | tf_op jit(solution)/shard_map/rkab,kcbd->rcad/dot_general | solution.py:32
  964.9 2.3 gather_fusion.2
  967.2 374.3 %all-gather.13.cloned.1.call-done = f32[8,1,1,10,256,256]{5,4,3,2,1,0:T(8,128)} async-done(((f32[1,1,1,10,256,256]{5,4,3,2,1,0:T(8,128)}), f32[8,1,1,10,256,256]{5,4,3,2,1,0:T(8,128)}) %all-gather.13.cloned.1.call-update) | async-done | bytes 20971536 | tf_op jit(solution)/shard_map/all_gather | solution.py:20
  1341.5 8.2 reduce_sum.73
  1349.7 4.5 fusion.20
  1354.2 20.4 %fusion.44 = f32[3,4,256,256]{2,3,0,1:T(8,128)S(1)} fusion(f32[3,4,256,256]{3,1,2,0:T(4,128)S(1)} %fusion.20, f32[4,4,256,256,1]{3,1,2,0,4:T(4,128)S(1)} %copy-done), kind=kOutput, calls=%fused_computation.41 | convolution fusion | flops 9663676416 | bytes 10485760 | tf_op jit(solution)/shard_map/rkab,kcbd->rcad/dot_general | solution.py:32
  1374.6 2.3 gather_fusion
  1376.9 374.1 %all-gather.15.cloned.1.call-done = f32[8,1,1,10,256,256]{5,4,3,2,1,0:T(8,128)} async-done(((f32[1,1,1,10,256,256]{5,4,3,2,1,0:T(8,128)}), f32[8,1,1,10,256,256]{5,4,3,2,1,0:T(8,128)}) %all-gather.15.cloned.1.call-update) | async-done | bytes 20971536 | tf_op jit(solution)/shard_map/all_gather | solution.py:20
  1751.0 8.2 reduce_sum.75
  1759.2 4.4 fusion.16
  1763.6 20.2 %fusion.49 = f32[3,4,256,256]{2,3,0,1:T(8,128)S(1)} fusion(f32[3,4,256,256]{3,1,2,0:T(4,128)S(1)} %fusion.16, f32[4,4,256,256,1]{3,1,2,0,4:T(4,128)S(1)} %copy-done.1), kind=kOutput, calls=%fused_computation.42 | convolution fusion | flops 9663676416 | bytes 10485760 | tf_op jit(solution)/shard_map/rkab,kcbd->rcad/dot_general | solution.py:32
  1783.8 2.3 gather_fusion.1
  1786.2 4.9 add_bitcast_fusion
  1791.0 2.1 copy.8
  (62 shorter events, 1.6 us)
Async XLA Ops:
  6.5 514.8 %all-gather.19.cloned.1.call-start = ((), (), s32[]{:S(2)}) async-start(), calls=%async_computation.3 | async-start | bytes 23592960 | tf_op jit(solution)/shard_map/all_gather | solution.py:20
  16.6 915.2 %all-gather.17.cloned.1.call-start = ((), (), s32[]{:S(2)}) async-start(), calls=%async_computation.2 | async-start | bytes 23592960 | tf_op jit(solution)/shard_map/all_gather | solution.py:20
  17.4 1.9 copy-start.4
  17.4 5.1 copy-start.5
  17.4 11.1 copy-start.6
  17.4 1324.1 %all-gather.13.cloned.1.call-start = ((), (), s32[]{:S(2)}) async-start(), calls=%async_computation | async-start | bytes 23592960 | tf_op jit(solution)/shard_map/all_gather | solution.py:20
  18.2 1732.9 %all-gather.15.cloned.1.call-start = ((), (), s32[]{:S(2)}) async-start(), calls=%async_computation.1 | async-start | bytes 23592960 | tf_op jit(solution)/shard_map/all_gather | solution.py:20
  19.3 85.9 %collective-permute-start.1 = (f32[12,256,256]{2,1,0:T(8,128)S(1)}, f32[12,256,256]{2,1,0:T(8,128)}, u32[]{:S(2)}, u32[]{:S(2)}) collective-permute-start(f32[12,256,256]{2,1,0:T(8,128)S(1)} %bitcast.123), channel_id=1, source_target_pairs={{0,248},{8,0},{16,8},{24,16},{32,24},{40,32},{48,40},{56,48},{64,5... | collective-permute-start | bytes 9437192 | tf_op jit(solution)/shard_map/ppermute | solution.py:15
  22.5 240.0 %collective-permute-start = (f32[12,2]{0,1:T(2,128)S(1)}, f32[12,2]{0,1:T(2,128)S(1)}, u32[]{:S(2)}, u32[]{:S(2)}) collective-permute-start(f32[12,2]{0,1:T(2,128)S(1)} %get-tuple-element.20), channel_id=1, source_target_pairs={{0,248},{8,0},{16,8},{24,16},{32,24},{40,32},{48,40},{56,48},{64,5... | collective-permute-start | bytes 296 | tf_op jit(solution)/shard_map/ppermute | solution.py:15
  105.2 151.0 %collective-permute-start.3 = (f32[12,256,256]{2,1,0:T(8,128)}, f32[12,256,256]{2,1,0:T(8,128)}, u32[]{:S(2)}, u32[]{:S(2)}) collective-permute-start(f32[12,256,256]{2,1,0:T(8,128)} %collective-permute-done.1), channel_id=1, source_target_pairs={{0,248},{8,0},{16,8},{24,16},{32,24},{40,32},{48,40},{56,48},{64,5... | collective-permute-start | bytes 9437192 | tf_op jit(solution)/shard_map/ppermute | solution.py:15
  256.3 139.0 %collective-permute-start.5 = (f32[12,256,256]{2,1,0:T(8,128)}, f32[12,256,256]{2,1,0:T(8,128)S(1)}, u32[]{:S(2)}, u32[]{:S(2)}) collective-permute-start(f32[12,256,256]{2,1,0:T(8,128)} %collective-permute-done.3), channel_id=1, source_target_pairs={{0,248},{8,0},{16,8},{24,16},{32,24},{40,32},{48,40},{56,48},{64,5... | collective-permute-start | bytes 9437192 | tf_op jit(solution)/shard_map/ppermute | solution.py:15
  256.3 6.2 copy-start.7
  262.5 111.0 %collective-permute-start.2 = (f32[12,2]{0,1:T(2,128)S(1)}, f32[12,2]{0,1:T(2,128)S(1)}, u32[]{:S(2)}, u32[]{:S(2)}) collective-permute-start(f32[12,2]{0,1:T(2,128)S(1)} %collective-permute-done), channel_id=1, source_target_pairs={{0,248},{8,0},{16,8},{24,16},{32,24},{40,32},{48,40},{56,48},{64,5... | collective-permute-start | bytes 296 | tf_op jit(solution)/shard_map/ppermute | solution.py:15
  373.5 4.9 collective-permute-start.4
  529.5 4.4 copy-start.3
  940.0 4.7 copy-start.2
  1349.7 4.5 copy-start
  1759.2 4.4 copy-start.1
Sparse Core Ops, SparseCore 0:
  16.8 504.5 all-gather.18
  523.2 408.6 all-gather.16
  933.7 407.8 all-gather.12
  1343.2 407.8 all-gather.14
